TPU v7x, 32 devices: a whole 2x2x4 slice. The times are simulated.
32 devices in a mesh: grp: 2 (over y), gx: 4 (over z), gy: 2 (over x), gz: 2 (over core).
Axes of the slice: x: 2, y: 2, z: 4, core: 2. Of those that a mesh axis runs over, the one named last changes fastest.
Arguments:
- density: float32 [32, 256, 256], P(('grp', 'gz'), 'gx', 'gy'), parts along dimension 0, may hold values from -6 to 6
- sigma: float32 [32, 256, 256], P(('grp', 'gz'), 'gx', 'gy'), parts along dimension 0, may hold values from -6 to 6
- mt_values: bfloat16 [16, 8, 2, 16, 128], P(('grp', 'gx', 'gy'), None, None, 'gz'), parts along dimension 0, may hold values from -6 to 6
- mt_rows: int32 [16, 8, 2], P(('grp', 'gx', 'gy')), parts along dimension 0, may hold values from 0 to 63
- mt_counts: int32 [16, 8], P(('grp', 'gx', 'gy')), parts along dimension 0, may hold values from 0 to 2, as said below
- kernel: bfloat16 [6, 16, 17, 17], P(None, 'gz'), may hold values from -0.09375 to 0.09375
- observed: float32 [12, 256, 256], P('grp', 'gx', 'gy'), parts along dimension 0, may hold values from -6 to 6
Outputs:
- sigma_trial: float32 [32, 256, 256], P(('grp', 'gz'), 'gx', 'gy'), parts along dimension 0
- density_trial: float32 [32, 256, 256], P(('grp', 'gz'), 'gx', 'gy'), parts along dimension 0
- tensor_residual: float32 [12, 256, 256], P('grp', 'gx', 'gy'), parts along dimension 0
There are 2 independent parts, one for each index of `grp`. A program takes and returns all parts, laid end to end along the dimension named above; an argument that names none is the same for every part. Nothing has to cross between parts.
Inputs may be any that keep to these rules, and one draw needn't show every extreme that they name: `mt_counts`: some owner tile receives 2 used slots from every source tile.
All inputs are finite; a program needn't handle non-finite values.
Results may differ from a plain program's by a relative error of at most 0.002.
Values may be sent and summed in bfloat16 or wider, within the bound.
A program may use at most 64 MiB of HBM per device.

v0:
```python
import jax
import jax.numpy as jnp
from jax import lax
from jax.sharding import PartitionSpec as P

step_sigma = 0.5
step_density = 0.25


def padded_2(block, sides, width):
    for axis, dim in sides:
        count = lax.axis_size(axis)
        forward = [(i, i + 1) for i in range(count - 1)]
        backward = [(target, source) for source, target in forward]
        low = lax.ppermute(
            lax.slice_in_dim(block, block.shape[dim] - width, None, axis=dim), axis, forward
        )
        high = lax.ppermute(lax.slice_in_dim(block, 0, width, axis=dim), axis, backward)
        block = jnp.concatenate([low, block, high], axis=dim)
    return block


def central(padded):
    along_x = (padded[1:-1, 2:, 1:-1] - padded[1:-1, :-2, 1:-1]) * 0.5
    along_y = (padded[1:-1, 1:-1, 2:] - padded[1:-1, 1:-1, :-2]) * 0.5
    along_z = (padded[2:, 1:-1, 1:-1] - padded[:-2, 1:-1, 1:-1]) * 0.5
    return (along_x, along_y, along_z)


def crossed(first, second):
    return (
        first[1] * second[2] - first[2] * second[1],
        first[2] * second[0] - first[0] * second[2],
        first[0] * second[1] - first[1] * second[0],
    )


def divergence(padded):
    part_x = padded[0, 1:-1, 2:, 1:-1] - padded[0, 1:-1, :-2, 1:-1]
    part_y = padded[1, 1:-1, 1:-1, 2:] - padded[1, 1:-1, 1:-1, :-2]
    part_z = padded[2, 2:, 1:-1, 1:-1] - padded[2, :-2, 1:-1, 1:-1]
    return (part_x + part_y + part_z) * 0.5


def footprint(wide, kernel, row_count, column_count):
    span = kernel.shape[2]
    shifts = jnp.arange(span, dtype=jnp.int32)
    inputs = jnp.arange(column_count + span - 1, dtype=jnp.int32)
    outputs = jnp.arange(column_count, dtype=jnp.int32)
    select = (inputs[None, :, None] - outputs[None, None, :] == shifts[:, None, None]).astype(
        jnp.bfloat16
    )
    result = jnp.zeros((kernel.shape[0], row_count, column_count), jnp.float32)
    for offset in range(span):
        banded = jnp.einsum(
            "czb,bio->zico", kernel[:, :, offset, :], select, preferred_element_type=jnp.float32
        ).astype(jnp.bfloat16)
        result = result + jnp.einsum(
            "zxi,zico->cxo",
            wide[:, offset : offset + row_count, :],
            banded,
            preferred_element_type=jnp.float32,
        )
    return result


def local(density, sigma, mt_values, mt_rows, mt_counts, kernel, observed):
    layer_count, row_count, column_count = density.shape
    capacity = mt_values.shape[2]
    arrived, slot_rows, slot_counts = (
        lax.all_to_all(mt_values, ("gx", "gy"), split_axis=1, concat_axis=0, tiled=True),
        lax.all_to_all(mt_rows, ("gx", "gy"), split_axis=1, concat_axis=0, tiled=True),
        lax.all_to_all(mt_counts, ("gx", "gy"), split_axis=1, concat_axis=0, tiled=True),
    )
    arrived = arrived.reshape(-1, layer_count, column_count)
    slot_rows = slot_rows.reshape(-1)
    live = (jnp.arange(capacity, dtype=jnp.int32)[None, :] < slot_counts).reshape(-1)
    picks = (
        (slot_rows[:, None] == jnp.arange(row_count, dtype=jnp.int32)[None, :]) & live[:, None]
    ).astype(jnp.bfloat16)
    grad_sum = jnp.einsum("sr,szy->zry", picks, arrived, preferred_element_type=jnp.float32)
    sigma_trial = sigma - step_sigma * grad_sum
    fields = jnp.stack([density, sigma_trial])
    padded = padded_2(fields, (("gx", 2), ("gy", 3), ("gz", 1)), 1)
    grad_model = central(padded[0])
    grad_cond = central(padded[1])
    flux = jnp.stack(crossed(grad_cond, crossed(grad_model, grad_cond)))
    flux_padded = padded_2(flux, (("gx", 2), ("gy", 3), ("gz", 1)), 1)
    coupling = -2.0 * divergence(flux_padded)
    density_trial = density - step_density * coupling
    wide = padded_2(density_trial.astype(jnp.bfloat16), (("gx", 1), ("gy", 2)), 8)
    partial_tensor = footprint(wide, kernel, row_count, column_count)
    predicted = lax.psum(partial_tensor, "gz")
    return (sigma_trial, density_trial, predicted - observed)


def solution(mesh):
    placed = (
        P(("grp", "gz"), "gx", "gy"),
        P(("grp", "gz"), "gx", "gy"),
        P(("grp", "gx", "gy"), None, None, "gz", None),
        P(("grp", "gx", "gy"), None, None),
        P(("grp", "gx", "gy"), None),
        P(None, "gz", None, None),
        P("grp", "gx", "gy"),
    )
    return jax.shard_map(
        local,
        mesh=mesh,
        in_specs=placed,
        out_specs=(
            P(("grp", "gz"), "gx", "gy"),
            P(("grp", "gz"), "gx", "gy"),
            P("grp", "gx", "gy"),
        ),
        check_vma=False,
    )
```

profile of v0, /device:TPU:0, one launch (start us, length us, event | category | flops | bytes accessed | tf_op | source)
XLA Modules:
  0.0 188.7 jit_solution(2979634791270995016)
XLA Ops:
  8.5 7.3 %all-to-all-start.1 = ((s32[1,8,1]{2,0,1:T(1,128)}), s32[1,8,1]{2,0,1:T(1,128)S(1)}, u32[]{:S(2)}, u32[]{:S(2)}) async-start(s32[1,8,1]{2,0,1:T(1,128)} %copy.63), calls=%async_computation.1 | async-start | bytes 8192 | tf_op jit(solution)/shard_map/all_to_all | solution.py:73
  17.1 5.0 %all-to-all-done.1 = s32[1,8,1]{2,0,1:T(1,128)S(1)} async-done(((s32[1,8,1]{2,0,1:T(1,128)}), s32[1,8,1]{2,0,1:T(1,128)S(1)}, u32[]{:S(2)}, u32[]{:S(2)}) %all-to-all-start.1) | async-done | bytes 64 | tf_op jit(solution)/shard_map/all_to_all | solution.py:73
  22.1 3.3 %all-to-all-start = ((s32[1,8,2]{2,0,1:T(1,128)}), s32[1,8,2]{2,0,1:T(1,128)S(1)}, u32[]{:S(2)}, u32[]{:S(2)}) async-start(s32[1,8,2]{2,0,1:T(1,128)} %copy.62), calls=%async_computation | async-start | bytes 8192 | tf_op jit(solution)/shard_map/all_to_all | solution.py:72
  25.7 6.1 %all-to-all-done = s32[1,8,2]{2,0,1:T(1,128)S(1)} async-done(((s32[1,8,2]{2,0,1:T(1,128)}), s32[1,8,2]{2,0,1:T(1,128)S(1)}, u32[]{:S(2)}, u32[]{:S(2)}) %all-to-all-start) | async-done | bytes 96 | tf_op jit(solution)/shard_map/all_to_all | solution.py:72
  31.8 3.3 %all-to-all-start.2 = ((bf16[1,8,2,8,128]{4,3,2,0,1:T(8,128)(2,1)}), bf16[1,8,2,8,128]{4,3,2,0,1:T(8,128)(2,1)S(1)}, u32[]{:S(2)}, u32[]{:S(2)}) async-start(bf16[1,8,2,8,128]{4,3,2,0,1:T(8,128)(2,1)} %bitcast.501), calls=%async_computation.2 | async-start | bytes 65536 | tf_op jit(solution)/shard_map/all_to_all | solution.py:71
  36.6 5.1 %all-to-all-done.2 = bf16[1,8,2,8,128]{4,3,2,0,1:T(8,128)(2,1)S(1)} async-done(((bf16[1,8,2,8,128]{4,3,2,0,1:T(8,128)(2,1)}), bf16[1,8,2,8,128]{4,3,2,0,1:T(8,128)(2,1)S(1)}, u32[]{:S(2)}, u32[]{:S(2)}) %all-to-all-start.2) | async-done | bytes 32800 | tf_op jit(solution)/shard_map/all_to_all | solution.py:71
  45.2 4.5 %collective-permute-start = (f32[2,8,1,128]{3,2,1,0:T(1,128)S(1)}, f32[2,8,1,128]{3,2,1,0:T(1,128)S(1)}, u32[]{:S(2)}, u32[]{:S(2)}) collective-permute-start(f32[2,8,1,128]{3,2,1,0:T(1,128)S(1)} %get-tuple-element.17), channel_id=1, source_target_pairs={{0,4},{4,8},{8,12},{1,5},{5,9},{9,13},{2,6},{6,10},{10,14},{3,7},{... | collective-permute-start | bytes 24584 | tf_op jit(solution)/shard_map/ppermute | solution.py:15
  54.1 4.5 %collective-permute-start.2 = (f32[2,8,66,1]{2,1,3,0:T(8,128)S(1)}, f32[2,8,66,1]{2,1,3,0:T(8,128)S(1)}, u32[]{:S(2)}, u32[]{:S(2)}) collective-permute-start(f32[2,8,66,1]{2,1,3,0:T(8,128)S(1)} %copy.66), channel_id=1, source_target_pairs={{0,2},{1,3},{4,6},{5,7},{8,10},{9,11},{12,14},{13,15},{16,18},{17,... | collective-permute-start | bytes 12680 | tf_op jit(solution)/shard_map/ppermute | solution.py:15
  61.9 3.0 %collective-permute-start.4 = (f32[2,1,66,130]{3,2,1,0:T(8,128)S(1)}, f32[2,1,66,130]{3,2,1,0:T(8,128)S(1)}, u32[]{:S(2)}, u32[]{:S(2)}) collective-permute-start(f32[2,1,66,130]{3,2,1,0:T(8,128)S(1)} %get-tuple-element.7), channel_id=1, source_target_pairs={{0,1},{2,3},{4,5},{6,7},{8,9},{10,11},{12,13},{14,15},{16,17},{18,... | collective-permute-start | bytes 205928 | tf_op jit(solution)/shard_map/ppermute | solution.py:15
  70.2 4.8 %collective-permute-start.7 = (f32[3,8,1,128]{3,2,1,0:T(1,128)S(1)}, f32[3,8,1,128]{3,2,1,0:T(1,128)S(1)}, u32[]{:S(2)}, u32[]{:S(2)}) collective-permute-start(f32[3,8,1,128]{3,2,1,0:T(1,128)S(1)} %get-tuple-element.13), channel_id=1, source_target_pairs={{0,4},{4,8},{8,12},{1,5},{5,9},{9,13},{2,6},{6,10},{10,14},{3,7},{... | collective-permute-start | bytes 36872 | tf_op jit(solution)/shard_map/ppermute | solution.py:15
  78.8 4.5 %collective-permute-start.9 = (f32[3,8,66,1]{2,1,3,0:T(8,128)S(1)}, f32[3,8,66,1]{2,1,3,0:T(8,128)S(1)}, u32[]{:S(2)}, u32[]{:S(2)}) collective-permute-start(f32[3,8,66,1]{2,1,3,0:T(8,128)S(1)} %copy.72), channel_id=1, source_target_pairs={{0,2},{1,3},{4,6},{5,7},{8,10},{9,11},{12,14},{13,15},{16,18},{17,... | collective-permute-start | bytes 19016 | tf_op jit(solution)/shard_map/ppermute | solution.py:15
  88.1 2.1 %collective-permute-done.10 = f32[3,1,66,130]{3,2,1,0:T(8,128)S(1)} collective-permute-done((f32[3,1,66,130]{3,2,1,0:T(8,128)S(1)}, f32[3,1,66,130]{3,2,1,0:T(8,128)S(1)}, u32[]{:S(2)}, u32[]{:S(2)}) %collective-permute-start.10) | collective-permute-done | bytes 102992 | tf_op jit(solution)/shard_map/ppermute | solution.py:18
  92.6 4.8 %collective-permute-start.12 = (bf16[8,8,128]{2,1,0:T(8,128)(2,1)S(1)}, bf16[8,8,128]{2,1,0:T(8,128)(2,1)S(1)}, u32[]{:S(2)}, u32[]{:S(2)}) collective-permute-start(bf16[8,8,128]{2,1,0:T(8,128)(2,1)S(1)} %get-tuple-element.38), channel_id=1, source_target_pairs={{0,4},{4,8},{8,12},{1,5},{5,9},{9,13},{2,6},{6,10},{10,14},{3,7},{... | collective-permute-start | bytes 49160 | tf_op jit(solution)/shard_map/ppermute | solution.py:15
  100.3 4.7 %collective-permute-start.14 = (bf16[8,80,8]{2,1,0:T(8,128)(2,1)S(1)}, bf16[8,80,8]{2,1,0:T(8,128)(2,1)S(1)}, u32[]{:S(2)}, u32[]{:S(2)}) collective-permute-start(bf16[8,80,8]{2,1,0:T(8,128)(2,1)S(1)} %get-tuple-element.36), channel_id=1, source_target_pairs={{0,2},{1,3},{4,6},{5,7},{8,10},{9,11},{12,14},{13,15},{16,18},{17,... | collective-permute-start | bytes 30728 | tf_op jit(solution)/shard_map/ppermute | solution.py:15
  107.9 1.8 slice_bitcast_fusion.18
  109.7 1.9 copy.127
  111.6 1.9 %copy.126 = bf16[8,64,144,1]{1,0,3,2:T(8,128)(2,1)} copy(bf16[8,64,144,1]{2,1,0,3:T(8,128)(2,1)} %get-tuple-element.21) | data formatting | bytes 294912 | tf_op jit(solution)/shard_map/slice | solution.py:60
  113.5 2.5 %fusion.287 = f32[6,128,64]{1,2,0:T(8,128)} fusion(bf16[8,64,144,1]{1,0,3,2:T(8,128)(2,1)} %copy.127, s32[144,128]{1,0:T(8,128)S(1)} %iota_subtract_fusion, bf16[6,8,17,17]{3,1,2,0:T(8,128)(2,1)} %param.12), kind=kOutput, calls=%fused_computation.111 | convolution fusion | flops 144525312 | bytes 577536 | tf_op jit(solution)/shard_map/zxi,zico->cxo/dot_general | solution.py:58
  116.0 2.5 %fusion.282 = f32[6,128,64]{1,2,0:T(8,128)} fusion(bf16[8,64,144,1]{1,0,3,2:T(8,128)(2,1)} %copy.126, s32[144,128]{1,0:T(8,128)S(1)} %iota_subtract_fusion, bf16[6,8,17,17]{3,1,2,0:T(8,128)(2,1)} %param.12), kind=kOutput, calls=%fused_computation.110 | convolution fusion | flops 144525312 | bytes 577536 | tf_op jit(solution)/shard_map/zxi,zico->cxo/dot_general | solution.py:58
  118.5 1.9 copy.125
  120.4 2.5 %fusion.277 = f32[6,128,64]{1,2,0:T(8,128)} fusion(bf16[8,64,144,1]{1,0,3,2:T(8,128)(2,1)} %copy.125, s32[144,128]{1,0:T(8,128)S(1)} %iota_subtract_fusion, bf16[6,8,17,17]{3,1,2,0:T(8,128)(2,1)} %param.12), kind=kOutput, calls=%fused_computation.109 | convolution fusion | flops 144525312 | bytes 577536 | tf_op jit(solution)/shard_map/zxi,zico->cxo/dot_general | solution.py:58
  122.9 1.9 copy.124
  124.7 2.5 %fusion.272 = f32[6,128,64]{1,2,0:T(8,128)} fusion(bf16[8,64,144,1]{1,0,3,2:T(8,128)(2,1)} %copy.124, s32[144,128]{1,0:T(8,128)S(1)} %iota_subtract_fusion, bf16[6,8,17,17]{3,1,2,0:T(8,128)(2,1)} %param.12), kind=kOutput, calls=%fused_computation.108 | convolution fusion | flops 144525312 | bytes 577536 | tf_op jit(solution)/shard_map/zxi,zico->cxo/dot_general | solution.py:58
  128.2 2.5 %fusion.267 = f32[6,128,64]{1,2,0:T(8,128)} fusion(bf16[8,64,144,1]{1,0,3,2:T(8,128)(2,1)} %copy.123, s32[144,128]{1,0:T(8,128)S(1)} %iota_subtract_fusion, bf16[6,8,17,17]{3,1,2,0:T(8,128)(2,1)} %param.12), kind=kOutput, calls=%fused_computation.107 | convolution fusion | flops 144525312 | bytes 577536 | tf_op jit(solution)/shard_map/zxi,zico->cxo/dot_general | solution.py:58
  130.9 2.3 %fusion.262 = f32[6,128,64]{1,2,0:T(8,128)} fusion(bf16[8,64,144,1]{1,0,3,2:T(8,128)(2,1)S(1)} %copy.122, s32[144,128]{1,0:T(8,128)S(1)} %iota_subtract_fusion, bf16[6,8,17,17]{3,1,2,0:T(8,128)(2,1)} %param.12), kind=kOutput, calls=%fused_computation.106 | convolution fusion | flops 144525312 | bytes 430080 | tf_op jit(solution)/shard_map/zxi,zico->cxo/dot_general | solution.py:58
  142.5 2.2 %fusion.232 = f32[6,128,64]{1,2,0:T(8,128)} fusion(bf16[8,64,144,1]{1,0,3,2:T(8,128)(2,1)S(1)} %copy.116, s32[144,128]{1,0:T(8,128)S(1)} %iota_subtract_fusion, bf16[6,8,17,17]{3,1,2,0:T(8,128)(2,1)} %param.12), kind=kOutput, calls=%fused_computation.100 | convolution fusion | flops 144525312 | bytes 430080 | tf_op jit(solution)/shard_map/zxi,zico->cxo/dot_general | solution.py:58
  145.0 2.2 %fusion.227 = f32[6,128,64]{1,2,0:T(8,128)} fusion(bf16[8,64,144,1]{1,0,3,2:T(8,128)(2,1)S(1)} %copy.115, s32[144,128]{1,0:T(8,128)S(1)} %iota_subtract_fusion, bf16[6,8,17,17]{3,1,2,0:T(8,128)(2,1)} %param.12), kind=kOutput, calls=%fused_computation.99 | convolution fusion | flops 144525312 | bytes 430080 | tf_op jit(solution)/shard_map/zxi,zico->cxo/dot_general | solution.py:58
  147.5 2.2 %fusion.222 = f32[6,128,64]{1,2,0:T(8,128)} fusion(bf16[8,64,144,1]{1,0,3,2:T(8,128)(2,1)S(1)} %copy.114, s32[144,128]{1,0:T(8,128)S(1)} %iota_subtract_fusion, bf16[6,8,17,17]{3,1,2,0:T(8,128)(2,1)} %param.12), kind=kOutput, calls=%fused_computation.98 | convolution fusion | flops 144525312 | bytes 430080 | tf_op jit(solution)/shard_map/zxi,zico->cxo/dot_general | solution.py:58
  149.9 2.2 %fusion.217 = f32[6,128,64]{1,2,0:T(8,128)} fusion(bf16[8,64,144,1]{1,0,3,2:T(8,128)(2,1)S(1)} %copy.113, s32[144,128]{1,0:T(8,128)S(1)} %iota_subtract_fusion, bf16[6,8,17,17]{3,1,2,0:T(8,128)(2,1)} %param.12), kind=kOutput, calls=%fused_computation.97 | convolution fusion | flops 144525312 | bytes 430080 | tf_op jit(solution)/shard_map/zxi,zico->cxo/dot_general | solution.py:58
  152.4 2.4 %fusion.212 = f32[6,128,64]{1,2,0:T(8,128)} fusion(bf16[8,64,144,1]{1,0,3,2:T(8,128)(2,1)S(1)} %copy.112, s32[144,128]{1,0:T(8,128)S(1)} %iota_subtract_fusion, bf16[6,8,17,17]{3,1,2,0:T(8,128)(2,1)} %param.12), kind=kOutput, calls=%fused_computation.96 | convolution fusion | flops 144525312 | bytes 430080 | tf_op jit(solution)/shard_map/zxi,zico->cxo/dot_general | solution.py:58
  155.2 3.0 %fusion.207 = f32[6,64,128]{2,1,0:T(8,128)} fusion(f32[6,128,64]{1,2,0:T(8,128)S(1)} %copy-done.2, f32[6,128,64]{1,2,0:T(8,128)S(1)} %copy-done.3, f32[6,128,64]{1,2,0:T(8,128)S(1)} %copy-done.4, f32[6,128,64]{1,2,0:T(8,128)S(1)} %copy-done.5, f32[6,128,64]{1,2,0:T(8,128)S(1)} %copy-done.6, f32[6,128,64]{1,2,0:T(8,128)S(1)} %copy-done.7, ...), kind=kOutput, calls=%fused_computation.95 | convolution fusion | flops 145311744 | bytes 3575808 | tf_op jit(solution)/shard_map/zxi,zico->cxo/dot_general | solution.py:58
  158.2 22.1 %all-reduce.2.cloned.1.call-done = f32[6,64,128]{2,1,0:T(8,128)} async-done(((f32[6,64,128]{2,1,0:T(8,128)}), f32[6,64,128]{2,1,0:T(8,128)}) %all-reduce.2.cloned.1.call-update) | async-done | bytes 196624 | tf_op jit(solution)/shard_map/psum | solution.py:93
  (100 shorter events, 50.2 us)
Async XLA Ops:
  8.5 13.6 %all-to-all-start.1 = ((s32[1,8,1]{2,0,1:T(1,128)}), s32[1,8,1]{2,0,1:T(1,128)S(1)}, u32[]{:S(2)}, u32[]{:S(2)}) async-start(s32[1,8,1]{2,0,1:T(1,128)} %copy.63), calls=%async_computation.1 | async-start | bytes 8192 | tf_op jit(solution)/shard_map/all_to_all | solution.py:73
  22.1 9.6 %all-to-all-start = ((s32[1,8,2]{2,0,1:T(1,128)}), s32[1,8,2]{2,0,1:T(1,128)S(1)}, u32[]{:S(2)}, u32[]{:S(2)}) async-start(s32[1,8,2]{2,0,1:T(1,128)} %copy.62), calls=%async_computation | async-start | bytes 8192 | tf_op jit(solution)/shard_map/all_to_all | solution.py:72
  31.8 10.0 %all-to-all-start.2 = ((bf16[1,8,2,8,128]{4,3,2,0,1:T(8,128)(2,1)}), bf16[1,8,2,8,128]{4,3,2,0,1:T(8,128)(2,1)S(1)}, u32[]{:S(2)}, u32[]{:S(2)}) async-start(bf16[1,8,2,8,128]{4,3,2,0,1:T(8,128)(2,1)} %bitcast.501), calls=%async_computation.2 | async-start | bytes 65536 | tf_op jit(solution)/shard_map/all_to_all | solution.py:71
  35.1 145.1 %all-reduce.2.cloned.1.call-start = ((), (), s32[]{:S(2)}) async-start(), calls=%async_computation.3 | async-start | bytes 393216 | tf_op jit(solution)/shard_map/psum | solution.py:93
  43.0 22.9 %copy-start.1 = (f32[8,64,128]{2,1,0:T(8,128)}, f32[8,64,128]{2,1,0:T(8,128)S(1)}, u32[]{:S(2)}) copy-start(f32[8,64,128]{2,1,0:T(8,128)S(1)} %fusion.121) | copy-start | bytes 786436
  43.9 5.9 %collective-permute-start.1 = (f32[2,8,1,128]{3,2,1,0:T(1,128)S(1)}, f32[2,8,1,128]{3,2,1,0:T(1,128)S(1)}, u32[]{:S(2)}, u32[]{:S(2)}) collective-permute-start(f32[2,8,1,128]{3,2,1,0:T(1,128)S(1)} %get-tuple-element.18), channel_id=1, source_target_pairs={{4,0},{8,4},{12,8},{5,1},{9,5},{13,9},{6,2},{10,6},{14,10},{7,3},{... | collective-permute-start | bytes 24584 | tf_op jit(solution)/shard_map/ppermute | solution.py:18
  45.2 5.9 %collective-permute-start = (f32[2,8,1,128]{3,2,1,0:T(1,128)S(1)}, f32[2,8,1,128]{3,2,1,0:T(1,128)S(1)}, u32[]{:S(2)}, u32[]{:S(2)}) collective-permute-start(f32[2,8,1,128]{3,2,1,0:T(1,128)S(1)} %get-tuple-element.17), channel_id=1, source_target_pairs={{0,4},{4,8},{8,12},{1,5},{5,9},{9,13},{2,6},{6,10},{10,14},{3,7},{... | collective-permute-start | bytes 24584 | tf_op jit(solution)/shard_map/ppermute | solution.py:15
  52.3 8.0 %copy-start = (f32[8,64,128]{2,1,0:T(8,128)S(1)}, f32[8,64,128]{2,1,0:T(8,128)}, u32[]{:S(2)}) copy-start(f32[8,64,128]{2,1,0:T(8,128)} %param.7) | copy-start | bytes 786436
  52.6 6.1 %collective-permute-start.3 = (f32[2,8,66,1]{2,1,3,0:T(8,128)S(1)}, f32[2,8,66,1]{2,1,3,0:T(8,128)S(1)}, u32[]{:S(2)}, u32[]{:S(2)}) collective-permute-start(f32[2,8,66,1]{2,1,3,0:T(8,128)S(1)} %copy.67), channel_id=1, source_target_pairs={{2,0},{3,1},{6,4},{7,5},{10,8},{11,9},{14,12},{15,13},{18,16},{19,... | collective-permute-start | bytes 12680 | tf_op jit(solution)/shard_map/ppermute | solution.py:18
  54.1 5.9 %collective-permute-start.2 = (f32[2,8,66,1]{2,1,3,0:T(8,128)S(1)}, f32[2,8,66,1]{2,1,3,0:T(8,128)S(1)}, u32[]{:S(2)}, u32[]{:S(2)}) collective-permute-start(f32[2,8,66,1]{2,1,3,0:T(8,128)S(1)} %copy.66), channel_id=1, source_target_pairs={{0,2},{1,3},{4,6},{5,7},{8,10},{9,11},{12,14},{13,15},{16,18},{17,... | collective-permute-start | bytes 12680 | tf_op jit(solution)/shard_map/ppermute | solution.py:15
  60.6 4.4 %collective-permute-start.5 = (f32[2,1,66,130]{3,2,1,0:T(8,128)S(1)}, f32[2,1,66,130]{3,2,1,0:T(8,128)S(1)}, u32[]{:S(2)}, u32[]{:S(2)}) collective-permute-start(f32[2,1,66,130]{3,2,1,0:T(8,128)S(1)} %get-tuple-element.8), channel_id=1, source_target_pairs={{1,0},{3,2},{5,4},{7,6},{9,8},{11,10},{13,12},{15,14},{17,16},{19,... | collective-permute-start | bytes 205928 | tf_op jit(solution)/shard_map/ppermute | solution.py:18
  61.9 4.0 %collective-permute-start.4 = (f32[2,1,66,130]{3,2,1,0:T(8,128)S(1)}, f32[2,1,66,130]{3,2,1,0:T(8,128)S(1)}, u32[]{:S(2)}, u32[]{:S(2)}) collective-permute-start(f32[2,1,66,130]{3,2,1,0:T(8,128)S(1)} %get-tuple-element.7), channel_id=1, source_target_pairs={{0,1},{2,3},{4,5},{6,7},{8,9},{10,11},{12,13},{14,15},{16,17},{18,... | collective-permute-start | bytes 205928 | tf_op jit(solution)/shard_map/ppermute | solution.py:15
  68.9 6.1 %collective-permute-start.6 = (f32[3,8,1,128]{3,2,1,0:T(1,128)S(1)}, f32[3,8,1,128]{3,2,1,0:T(1,128)S(1)}, u32[]{:S(2)}, u32[]{:S(2)}) collective-permute-start(f32[3,8,1,128]{3,2,1,0:T(1,128)S(1)} %get-tuple-element.14), channel_id=1, source_target_pairs={{4,0},{8,4},{12,8},{5,1},{9,5},{13,9},{6,2},{10,6},{14,10},{7,3},{... | collective-permute-start | bytes 36872 | tf_op jit(solution)/shard_map/ppermute | solution.py:18
  70.2 6.2 %collective-permute-start.7 = (f32[3,8,1,128]{3,2,1,0:T(1,128)S(1)}, f32[3,8,1,128]{3,2,1,0:T(1,128)S(1)}, u32[]{:S(2)}, u32[]{:S(2)}) collective-permute-start(f32[3,8,1,128]{3,2,1,0:T(1,128)S(1)} %get-tuple-element.13), channel_id=1, source_target_pairs={{0,4},{4,8},{8,12},{1,5},{5,9},{9,13},{2,6},{6,10},{10,14},{3,7},{... | collective-permute-start | bytes 36872 | tf_op jit(solution)/shard_map/ppermute | solution.py:15
  77.2 6.2 %collective-permute-start.8 = (f32[3,8,66,1]{2,1,3,0:T(8,128)S(1)}, f32[3,8,66,1]{2,1,3,0:T(8,128)S(1)}, u32[]{:S(2)}, u32[]{:S(2)}) collective-permute-start(f32[3,8,66,1]{2,1,3,0:T(8,128)S(1)} %copy.70), channel_id=1, source_target_pairs={{2,0},{3,1},{6,4},{7,5},{10,8},{11,9},{14,12},{15,13},{18,16},{19,... | collective-permute-start | bytes 19016 | tf_op jit(solution)/shard_map/ppermute | solution.py:18
  78.8 5.9 %collective-permute-start.9 = (f32[3,8,66,1]{2,1,3,0:T(8,128)S(1)}, f32[3,8,66,1]{2,1,3,0:T(8,128)S(1)}, u32[]{:S(2)}, u32[]{:S(2)}) collective-permute-start(f32[3,8,66,1]{2,1,3,0:T(8,128)S(1)} %copy.72), channel_id=1, source_target_pairs={{0,2},{1,3},{4,6},{5,7},{8,10},{9,11},{12,14},{13,15},{16,18},{17,... | collective-permute-start | bytes 19016 | tf_op jit(solution)/shard_map/ppermute | solution.py:15
  85.5 2.6 %collective-permute-start.11 = (f32[3,1,66,130]{3,2,1,0:T(8,128)S(1)}, f32[3,1,66,130]{3,2,1,0:T(8,128)S(1)}, u32[]{:S(2)}, u32[]{:S(2)}) collective-permute-start(f32[3,1,66,130]{3,2,1,0:T(8,128)S(1)} %get-tuple-element.6), channel_id=1, source_target_pairs={{0,1},{2,3},{4,5},{6,7},{8,9},{10,11},{12,13},{14,15},{16,17},{18,... | collective-permute-start | bytes 308888 | tf_op jit(solution)/shard_map/ppermute | solution.py:15
  86.8 3.4 %collective-permute-start.10 = (f32[3,1,66,130]{3,2,1,0:T(8,128)S(1)}, f32[3,1,66,130]{3,2,1,0:T(8,128)S(1)}, u32[]{:S(2)}, u32[]{:S(2)}) collective-permute-start(f32[3,1,66,130]{3,2,1,0:T(8,128)S(1)} %get-tuple-element.5), channel_id=1, source_target_pairs={{1,0},{3,2},{5,4},{7,6},{9,8},{11,10},{13,12},{15,14},{17,16},{19,... | collective-permute-start | bytes 308888 | tf_op jit(solution)/shard_map/ppermute | solution.py:18
  91.3 6.1 %collective-permute-start.13 = (bf16[8,8,128]{2,1,0:T(8,128)(2,1)S(1)}, bf16[8,8,128]{2,1,0:T(8,128)(2,1)S(1)}, u32[]{:S(2)}, u32[]{:S(2)}) collective-permute-start(bf16[8,8,128]{2,1,0:T(8,128)(2,1)S(1)} %get-tuple-element.39), channel_id=1, source_target_pairs={{4,0},{8,4},{12,8},{5,1},{9,5},{13,9},{6,2},{10,6},{14,10},{7,3},{... | collective-permute-start | bytes 49160 | tf_op jit(solution)/shard_map/ppermute | solution.py:18
  92.6 6.3 %collective-permute-start.12 = (bf16[8,8,128]{2,1,0:T(8,128)(2,1)S(1)}, bf16[8,8,128]{2,1,0:T(8,128)(2,1)S(1)}, u32[]{:S(2)}, u32[]{:S(2)}) collective-permute-start(bf16[8,8,128]{2,1,0:T(8,128)(2,1)S(1)} %get-tuple-element.38), channel_id=1, source_target_pairs={{0,4},{4,8},{8,12},{1,5},{5,9},{9,13},{2,6},{6,10},{10,14},{3,7},{... | collective-permute-start | bytes 49160 | tf_op jit(solution)/shard_map/ppermute | solution.py:15
  99.0 7.3 %collective-permute-start.15 = (bf16[8,80,8]{2,1,0:T(8,128)(2,1)S(1)}, bf16[8,80,8]{2,1,0:T(8,128)(2,1)S(1)}, u32[]{:S(2)}, u32[]{:S(2)}) collective-permute-start(bf16[8,80,8]{2,1,0:T(8,128)(2,1)S(1)} %get-tuple-element.37), channel_id=1, source_target_pairs={{2,0},{3,1},{6,4},{7,5},{10,8},{11,9},{14,12},{15,13},{18,16},{19,... | collective-permute-start | bytes 30728 | tf_op jit(solution)/shard_map/ppermute | solution.py:18
  100.3 7.4 %collective-permute-start.14 = (bf16[8,80,8]{2,1,0:T(8,128)(2,1)S(1)}, bf16[8,80,8]{2,1,0:T(8,128)(2,1)S(1)}, u32[]{:S(2)}, u32[]{:S(2)}) collective-permute-start(bf16[8,80,8]{2,1,0:T(8,128)(2,1)S(1)} %get-tuple-element.36), channel_id=1, source_target_pairs={{0,2},{1,3},{4,6},{5,7},{8,10},{9,11},{12,14},{13,15},{16,18},{17,... | collective-permute-start | bytes 30728 | tf_op jit(solution)/shard_map/ppermute | solution.py:15
  152.2 2.9 %copy-start.2 = (f32[6,128,64]{1,2,0:T(8,128)S(1)}, f32[6,128,64]{1,2,0:T(8,128)}, u32[]{:S(2)}) copy-start(f32[6,128,64]{1,2,0:T(8,128)} %fusion.287) | copy-start | bytes 589828
  152.2 2.9 %copy-start.3 = (f32[6,128,64]{1,2,0:T(8,128)S(1)}, f32[6,128,64]{1,2,0:T(8,128)}, u32[]{:S(2)}) copy-start(f32[6,128,64]{1,2,0:T(8,128)} %fusion.282) | copy-start | bytes 589828
  152.2 2.9 %copy-start.4 = (f32[6,128,64]{1,2,0:T(8,128)S(1)}, f32[6,128,64]{1,2,0:T(8,128)}, u32[]{:S(2)}) copy-start(f32[6,128,64]{1,2,0:T(8,128)} %fusion.277) | copy-start | bytes 589828
  152.2 2.9 %copy-start.5 = (f32[6,128,64]{1,2,0:T(8,128)S(1)}, f32[6,128,64]{1,2,0:T(8,128)}, u32[]{:S(2)}) copy-start(f32[6,128,64]{1,2,0:T(8,128)} %fusion.272) | copy-start | bytes 589828
  152.2 2.9 %copy-start.6 = (f32[6,128,64]{1,2,0:T(8,128)S(1)}, f32[6,128,64]{1,2,0:T(8,128)}, u32[]{:S(2)}) copy-start(f32[6,128,64]{1,2,0:T(8,128)} %fusion.267) | copy-start | bytes 589828
  152.2 2.9 %copy-start.7 = (f32[6,128,64]{1,2,0:T(8,128)S(1)}, f32[6,128,64]{1,2,0:T(8,128)}, u32[]{:S(2)}) copy-start(f32[6,128,64]{1,2,0:T(8,128)} %fusion.262) | copy-start | bytes 589828
  155.2 25.1 %copy-start.8 = (f32[6,64,128]{2,1,0:T(8,128)S(1)}, f32[6,64,128]{2,1,0:T(8,128)}, u32[]{:S(2)}) copy-start(f32[6,64,128]{2,1,0:T(8,128)} %param.13) | copy-start | bytes 589828
Sparse Core Ops, SparseCore 0:
  158.3 21.9 all-reduce.1
where the time goes:
time: 190 us; the launch traced here: 189 us
  starting transfers between devices  56.7 us (30%)
  waiting for transfers between devices  50.1 us (26%)
  matrix products  38.2 us (20%)
  local copies, waits for them, and re-layouts  19.8 us (10%)
  between operations  14.6 us (8%)
  other arithmetic  9.27 us (5%)
    dot_general x17, matrix products, footprint(): jnp.einsum('zxi,zico->cxo', wide[:, offset:offset + row_count, :], banded...  37 us
    ppermute x8, starting transfers between devices, padded_2(): lax.ppermute(lax.slice_in_dim(block, block.shape[dim] - width, None, axis...  32.4 us
    psum x1, waiting for transfers between devices, local(): predicted = lax.psum(partial_tensor, 'gz')  22.1 us
    slice x18, local copies, waits for them, and re-layouts, footprint(): wide[:, offset:offset + row_count, :]  13.1 us
    ppermute x8, starting transfers between devices, padded_2(): lax.ppermute(lax.slice_in_dim(block, 0, width, axis=dim), axis, backward)  10.3 us
    ppermute x8, waiting for transfers between devices, padded_2(): lax.ppermute(lax.slice_in_dim(block, block.shape[dim] - width, None, axis...  8.48 us
    all_to_all x1, starting transfers between devices, local(): lax.all_to_all(mt_counts, ('gx', 'gy'), split_axis=1, concat_axis=0, tile...  7.25 us
    all_to_all x1, waiting for transfers between devices, local(): lax.all_to_all(mt_rows, ('gx', 'gy'), split_axis=1, concat_axis=0, tiled=...  6.09 us
  transfers between devices with their start and end apart: 20, of which 13 were waited for; matrix products, arithmetic and copies ran while one was open for 2% of the time, Pallas kernels for 0%

commit v1 on v0

v1 whole, which is shorter than its diff:
```python
import functools

import jax
import jax.numpy as jnp
from jax import lax
from jax.experimental import pallas as pl
from jax.experimental.pallas import tpu as pltpu
from jax.sharding import PartitionSpec as P

MESH = pl.DeviceIdType.MESH
STEPS = ((-1, 0), (1, 0), (0, -1), (0, 1), (-1, -1), (-1, 1), (1, -1), (1, 1))
EDGE = 8


def packed_columns(layers, half):
    lane = lax.broadcasted_iota(jnp.int32, layers[0].shape, 1)
    result = jnp.zeros_like(layers[0])
    for i, layer in enumerate(layers):
        result = jnp.where(lane // (2 * half) == i, pltpu.roll(layer, half + 2 * half * i, 1), result)
    return result


def halo_columns(left, right, i, half):
    lane = lax.broadcasted_iota(jnp.int32, left.shape, 1)
    own = 2 * half * i
    return jnp.where(
        lane < 64,
        pltpu.roll(right, (128 - own - half) % 128, 1),
        pltpu.roll(left, (128 - half - own) % 128, 1),
    )


def body(
    sizes, density_ref, sigma_ref, payload_ref, taps_ref, observed_ref,
    sigma_out, density_out, residual_out,
    arrived, wide_d, wide_s, pack, sides, flux_z, lateral, rounded, toeplitz, blocks, part, other,
    all_send, all_recv, z_send, z_recv, near_send, near_recv, sum_send, sum_recv,
):
    n_gx, n_gy, n_gz = sizes
    tiles = n_gx * n_gy
    nz, rows, cols = density_ref.shape
    comps = observed_ref.shape[0]
    span = taps_ref.shape[0] // comps
    ext = rows + 2 * EDGE
    ix, iy, iz = lax.axis_index("gx"), lax.axis_index("gy"), lax.axis_index("gz")
    me = ix * n_gy + iy
    inner = pl.ds(EDGE, rows)
    own = pl.ds(0, cols)

    def over_tiles(step):
        if tiles <= 16:
            for off in range(1, tiles):
                step(off)
        else:
            lax.fori_loop(1, tiles, lambda off, _: (step(off), 0)[1], 0)

    for wide in (wide_d, wide_s):
        wide[...] = jnp.zeros_like(wide)
    sides[...] = jnp.zeros_like(sides)
    rounded[...] = jnp.zeros_like(rounded)

    barrier = pltpu.get_barrier_semaphore()

    def greet(off):
        tile = lax.rem(me + off, tiles)
        pl.semaphore_signal(
            barrier, inc=1, device_id={"gx": tile // n_gy, "gy": lax.rem(tile, n_gy)}, device_id_type=MESH
        )

    over_tiles(greet)
    for off in range(1, n_gz):
        pl.semaphore_signal(barrier, inc=1, device_id={"gz": lax.rem(iz + off, n_gz)}, device_id_type=MESH)
    pl.semaphore_wait(barrier, tiles - 1 + n_gz - 1)

    def block_copy(tile, source):
        return pltpu.make_async_remote_copy(
            src_ref=payload_ref.at[tile], dst_ref=arrived.at[source],
            send_sem=all_send.at[tile], recv_sem=all_recv.at[source],
            device_id={"gx": tile // n_gy, "gy": lax.rem(tile, n_gy)}, device_id_type=MESH,
        )

    over_tiles(lambda off: block_copy(lax.rem(me + off, tiles), me).start())
    arrived[me] = payload_ref[me]

    def z_copy(wide, field, up):
        src, dst = (pl.ds(nz, 2), pl.ds(0, 2)) if up else (pl.ds(2, 2), pl.ds(nz + 2, 2))
        return pltpu.make_async_remote_copy(
            src_ref=wide.at[src, inner, own], dst_ref=wide.at[dst, inner, own],
            send_sem=z_send.at[field, int(up)], recv_sem=z_recv.at[field, int(up)],
            device_id={"gz": lax.rem(iz + (1 if up else n_gz - 1), n_gz)}, device_id_type=MESH,
        )

    has_up, has_down = iz < n_gz - 1, iz > 0

    def z_start(wide, field):
        pl.when(has_up)(lambda: z_copy(wide, field, True).start())
        pl.when(has_down)(lambda: z_copy(wide, field, False).start())

    def z_finish(wide, field):
        @pl.when(has_up)
        def _():
            z_copy(wide, field, True).wait_send()
            z_copy(wide, field, False).wait_recv()

        @pl.when(has_down)
        def _():
            z_copy(wide, field, False).wait_send()
            z_copy(wide, field, True).wait_recv()

    def inside(x, y):
        return (x >= 0) & (x < n_gx) & (y >= 0) & (y < n_gy)

    def near_copy(wide, field, at, dx, dy, x, y):
        if dy == 0:
            src = wide.at[:, pl.ds(EDGE if dx < 0 else rows, EDGE), own]
            dst = wide.at[:, pl.ds(EDGE + rows if dx < 0 else 0, EDGE), own]
        else:
            side = 0 if dy > 0 else 1
            source, target, count = {
                0: (0, EDGE, rows), -1: (0, EDGE + rows, EDGE), 1: (rows - EDGE, 0, EDGE)
            }[dx]
            src = pack.at[field, pl.ds(source, count)]
            dst = sides.at[field, side, pl.ds(target, count)]
        return pltpu.make_async_remote_copy(
            src_ref=src, dst_ref=dst, send_sem=near_send.at[field, at], recv_sem=near_recv.at[field, at],
            device_id={"gx": x, "gy": y}, device_id_type=MESH,
        )

    def near_start(wide, field):
        for at, (dx, dy) in enumerate(STEPS):
            @pl.when(inside(ix + dx, iy + dy))
            def _():
                near_copy(wide, field, at, dx, dy, ix + dx, iy + dy).start()

    def near_finish(wide, field):
        for at, (dx, dy) in enumerate(STEPS):
            @pl.when(inside(ix - dx, iy - dy))
            def _():
                near_copy(wide, field, at, dx, dy, ix - dx, iy - dy).wait_recv()

            @pl.when(inside(ix + dx, iy + dy))
            def _():
                near_copy(wide, field, at, dx, dy, ix + dx, iy + dy).wait_send()

    def unpack(wide, field):
        for i in range(nz + 4):
            wide[i, :, pl.ds(cols, cols)] = halo_columns(sides[field, 0], sides[field, 1], i, 4)

    wide_d[pl.ds(2, nz), inner, own] = density_ref[...]
    z_start(wide_d, 0)

    depth = taps_ref.shape[1]
    for row in range(span * comps):
        for half in range(depth // 128):
            taps = jnp.broadcast_to(taps_ref[row : row + 1, half * 128 : (half + 1) * 128], (16, 128))
            band = pltpu.roll(taps, 0, 1, stride=1, stride_axis=0)
            toeplitz[row * 16 : (row + 1) * 16, half * 128 : (half + 1) * 128] = band.astype(jnp.bfloat16)

    z_finish(wide_d, 0)
    pack[0] = packed_columns([wide_d[i, inner, own] for i in range(nz + 4)], 4)
    near_start(wide_d, 0)

    def landed(off):
        tile = lax.rem(me + off, tiles)
        copy = block_copy(tile, tile)
        copy.wait_recv()

    over_tiles(landed)
    slots = tiles * 16
    values = arrived[:, 0:16, :].reshape(slots, cols)
    picks = arrived[:, 16:32, :].reshape(slots, 128).astype(jnp.float32).T
    slot_z = lax.rem(lax.broadcasted_iota(jnp.int32, (128, slots), 1), nz)
    row_z = lax.broadcasted_iota(jnp.int32, (128, slots), 0) // rows
    for g in range(nz // 2):
        chosen = jnp.where(slot_z == row_z + 2 * g, picks, 0.0).astype(jnp.bfloat16)
        total = jnp.dot(chosen, values, preferred_element_type=jnp.float32)
        for j in range(2):
            trial = sigma_ref[2 * g + j] - 0.5 * total[j * rows : (j + 1) * rows]
            wide_s[2 * g + j + 2, inner, own] = trial
            sigma_out[2 * g + j] = trial
    z_start(wide_s, 1)
    near_finish(wide_d, 0)
    unpack(wide_d, 0)
    z_finish(wide_s, 1)
    pack[1] = packed_columns([wide_s[i, inner, own] for i in range(nz + 4)], 4)
    near_start(wide_s, 1)
    near_finish(wide_s, 1)
    unpack(wide_s, 1)

    at_row = lax.broadcasted_iota(jnp.int32, (ext, 2 * cols), 0)
    at_lane = lax.broadcasted_iota(jnp.int32, (ext, 2 * cols), 1)
    row_in = ((at_row >= EDGE) | (ix > 0)) & ((at_row < EDGE + rows) | (ix < n_gx - 1))
    lane_in = (at_lane < cols) | ((at_lane < cols + 64) & (iy < n_gy - 1)) | ((at_lane >= cols + 64) & (iy > 0))

    def shifted(value, axis):
        size = value.shape[axis]
        return pltpu.roll(value, size - 1, axis) - pltpu.roll(value, 1, axis)

    def layer(i, _):
        def gradient(wide):
            here = wide[i]
            return shifted(here, 0) * 0.5, shifted(here, 1) * 0.5, (wide[i + 1] - wide[i - 1]) * 0.5

        dx, dy, dz = gradient(wide_d)
        sx, sy, sz = gradient(wide_s)
        cx, cy, cz = dy * sz - dz * sy, dz * sx - dx * sz, dx * sy - dy * sx
        fx = jnp.where(row_in, sy * cz - sz * cy, 0.0)
        fy = jnp.where(lane_in, sz * cx - sx * cz, 0.0)
        fz = sx * cy - sy * cx
        z_in = ((i >= 2) | has_down) & ((i < nz + 2) | has_up)
        flux_z[i] = jnp.where(z_in, fz[EDGE : EDGE + rows, :cols], 0.0)
        lateral[i] = (shifted(fx, 0) + shifted(fy, 1))[EDGE : EDGE + rows, :cols]
        return 0

    lax.fori_loop(1, nz + 3, layer, 0)
    for i in range(nz):
        trial = density_ref[i] + 0.25 * (lateral[i + 2] + (flux_z[i + 3] - flux_z[i + 1]))
        density_out[i] = trial
        rounded[i, inner, own] = trial.astype(jnp.bfloat16).astype(jnp.float32)
    pack[2] = packed_columns([rounded[i, inner, own] for i in range(nz)], 8)
    near_start(rounded, 2)
    near_finish(rounded, 2)
    for i in range(nz):
        rounded[i, :, pl.ds(cols, cols)] = halo_columns(sides[2, 0], sides[2, 1], i, 8)

    for s in range(rows // 16):
        for i in range(nz):
            blocks[s, i * 32 : (i + 1) * 32, :] = rounded[i, s * 16 : s * 16 + 32, :].astype(jnp.bfloat16)

    def section(s, _):
        block = blocks[s]
        total = jnp.zeros((comps * 16, cols), jnp.float32)
        for b in range(span):
            one = jnp.dot(
                toeplitz[b * comps * 16 : (b + 1) * comps * 16, :], block, preferred_element_type=jnp.float32
            )
            total = total + pltpu.roll(one, (8 - b) % (2 * cols), 1)[:, :cols]
        for c in range(comps):
            part[c, pl.ds(pl.multiple_of(s * 16, 16), 16), :] = total[c * 16 : (c + 1) * 16]
        return 0

    lax.fori_loop(0, rows // 16, section, 0)

    if n_gz > 1:
        swap = pltpu.make_async_remote_copy(
            src_ref=part, dst_ref=other, send_sem=sum_send, recv_sem=sum_recv,
            device_id={"gz": n_gz - 1 - iz}, device_id_type=MESH,
        )
        swap.start()
        over_tiles(lambda off: block_copy(lax.rem(me + off, tiles), me).wait_send())
        swap.wait()
        residual_out[...] = part[...] + other[...] - observed_ref[...]
    else:
        over_tiles(lambda off: block_copy(lax.rem(me + off, tiles), me).wait_send())
        residual_out[...] = part[...] - observed_ref[...]


def local(sizes, density, sigma, mt_values, mt_rows, mt_counts, kernel, observed):
    nz, rows, cols = density.shape
    tiles, capacity = mt_values.shape[1:3]
    comps, span = kernel.shape[0], kernel.shape[2]
    ext = rows + 2 * EDGE
    live = jnp.arange(capacity, dtype=jnp.int32)[None, :] < mt_counts[0][:, None]
    target = jnp.where(live, mt_rows[0], -1)
    picks = target[:, :, None, None] == jnp.arange(128, dtype=jnp.int32) % rows
    picks = jnp.broadcast_to(picks, (tiles, capacity, nz, 128)).reshape(tiles, capacity * nz, 128)
    payload = jnp.concatenate(
        [mt_values[0].reshape(tiles, capacity * nz, cols), picks.astype(jnp.bfloat16)], axis=1
    )
    taps = jnp.pad(kernel.transpose(3, 0, 1, 2), ((0, 0), (0, 0), (0, 0), (0, 32 - span)))
    taps = taps.reshape(span * comps, nz * 32).astype(jnp.float32)
    vmem = pl.BlockSpec(memory_space=pltpu.VMEM)
    f32 = jnp.float32
    dma = pltpu.SemaphoreType.DMA
    return pl.pallas_call(
        functools.partial(body, sizes),
        out_shape=(
            jax.ShapeDtypeStruct(sigma.shape, f32),
            jax.ShapeDtypeStruct(density.shape, f32),
            jax.ShapeDtypeStruct(observed.shape, f32),
        ),
        in_specs=[vmem] * 5,
        out_specs=(vmem,) * 3,
        scratch_shapes=[
            pltpu.VMEM(payload.shape, jnp.bfloat16),
            pltpu.VMEM((nz + 4, ext, 2 * cols), f32),
            pltpu.VMEM((nz + 4, ext, 2 * cols), f32),
            pltpu.VMEM((3, rows, 128), f32),
            pltpu.VMEM((3, 2, ext, 128), f32),
            pltpu.VMEM((nz + 4, rows, cols), f32),
            pltpu.VMEM((nz + 4, rows, cols), f32),
            pltpu.VMEM((nz, ext, 2 * cols), f32),
            pltpu.VMEM((span * comps * 16, nz * 32), jnp.bfloat16),
            pltpu.VMEM((rows // 16, nz * 32, 2 * cols), jnp.bfloat16),
            pltpu.VMEM(observed.shape, f32),
            pltpu.VMEM(observed.shape, f32),
            dma((tiles,)), dma((tiles,)), dma((2, 2)), dma((2, 2)),
            dma((3, 8)), dma((3, 8)), dma, dma,
        ],
        compiler_params=pltpu.CompilerParams(
            collective_id=0, has_side_effects=True, vmem_limit_bytes=40 * 1024 * 1024
        ),
    )(density, sigma, payload, taps, observed)


def solution(mesh):
    field = P(("grp", "gz"), "gx", "gy")
    placed = (
        field,
        field,
        P(("grp", "gx", "gy"), None, None, "gz", None),
        P(("grp", "gx", "gy"), None, None),
        P(("grp", "gx", "gy"), None),
        P(None, "gz", None, None),
        P("grp", "gx", "gy"),
    )
    sizes = (mesh.shape["gx"], mesh.shape["gy"], mesh.shape["gz"])
    return jax.shard_map(
        functools.partial(local, sizes),
        mesh=mesh,
        in_specs=placed,
        out_specs=(field, field, P("grp", "gx", "gy")),
        check_vma=False,
    )
```

time: 190 us -> 32.4 us (0.17)
  starting transfers between devices: 56.7 us -> 0 us
  waiting for transfers between devices: 50.1 us -> 0 us
  matrix products: 38.2 us -> 0 us
  Pallas kernels: 0 us -> 26 us
  local copies, waits for them, and re-layouts: 19.8 us -> 4.61 us
  between operations: 14.6 us -> 0.71 us
  other arithmetic: 9.27 us -> 0.81 us
    ppermute x16 -> x0, starting transfers between devices: 42.7 us -> none  [the longest x8 32.4 us: padded_2(): lax.ppermute(lax.slice_in_dim(block, block.shape[dim] - width, None, axis...]
    dot_general x18 -> x0, matrix products: 38.2 us -> none  [the longest x17 37 us: footprint(): jnp.einsum('zxi,zico->cxo', wide[:, offset:offset + row_count, :], banded...]
    pallas_call x0 -> x1, Pallas kernels: none -> 26 us  [local(): pl.pallas_call(functools.partial(body, sizes), out_shape=(jax.ShapeDtypeS...]
    psum x1 -> x0, waiting for transfers between devices: 22.1 us -> none  [local(): predicted = lax.psum(partial_tensor, 'gz')]
    all_to_all x3 -> x0, waiting for transfers between devices: 16.3 us -> none  [the longest x1 6.09 us: local(): lax.all_to_all(mt_rows, ('gx', 'gy'), split_axis=1, concat_axis=0, tiled=...]
    slice x26 -> x0, local copies, waits for them, and re-layouts: 14.9 us -> none  [the longest x18 13.1 us: footprint(): wide[:, offset:offset + row_count, :]]
    all_to_all x3 -> x0, starting transfers between devices: 13.9 us -> none  [the longest x1 7.25 us: local(): lax.all_to_all(mt_counts, ('gx', 'gy'), split_axis=1, concat_axis=0, tile...]
    ppermute x16 -> x0, waiting for transfers between devices: 11.8 us -> none  [the longest x8 8.48 us: padded_2(): lax.ppermute(lax.slice_in_dim(block, block.shape[dim] - width, None, axis...]
  transfers between devices with their start and end apart: 20 -> 0, of which waited for: 13 -> 0; matrix products, arithmetic and copies ran while one was open for 2% -> 0% of each run, Pallas kernels for 0% -> 0%
where the time goes in v1:
time: 32.4 us; the launch traced here: 32.2 us
  Pallas kernels  26 us (80%)
  local copies, waits for them, and re-layouts  4.61 us (14%)
  other arithmetic  0.81 us (2%)
  between operations  0.71 us (2%)
    pallas_call x1, Pallas kernels, local(): pl.pallas_call(functools.partial(body, sizes), out_shape=(jax.ShapeDtypeS...  26 us
    unnamed x12, local copies, waits for them, and re-layouts  4.36 us
    select_n x1, other arithmetic, local(): target = jnp.where(live, mt_rows[0], -1)  0.69 us

profile of v1, /device:TPU:0, one launch (start us, length us, event | category | flops | bytes accessed | tf_op | source)
XLA Modules:
  0.0 32.2 jit_solution(6323700594123507145)
XLA Ops:
  0.6 0.0 copy-start.3
  0.7 0.7 %compare_select_fusion = s32[8,2]{0,1:T(2,128)S(1)} fusion(s32[1,8,2]{1,2,0:T(2,128)} %param.10, s32[8]{0:T(128)} %bitcast.11), kind=kLoop, calls=%fused_computation.5 | loop fusion | flops 32 | bytes 160 | tf_op jit(solution)/shard_map/jit(_where)/select_n | solution.py:264
  1.3 0.1 copy.12
  1.4 0.1 compare_convert_fusion
  1.5 0.0 copy-done.3
  1.5 1.4 %copy.13 = bf16[6,8,17,17]{2,1,0,3:T(8,128)(2,1)S(1)} copy(bf16[6,8,17,17]{3,1,2,0:T(8,128)(2,1)} %param.12) | data formatting | bytes 55488 | tf_op args[5]
  2.9 0.0 copy-start.2
  2.9 0.0 copy-start
  2.9 0.0 copy-start.1
  3.0 0.2 reshape.55.taps_ref
  3.1 0.7 %copy-done.2 = f32[6,64,128]{2,1,0:T(8,128)S(1)} copy-done((f32[6,64,128]{2,1,0:T(8,128)S(1)}, f32[6,64,128]{2,1,0:T(8,128)}, u32[]{:S(2)}) %copy-start.2) | copy-done | bytes 196632
  3.8 0.1 copy-done
  4.0 0.1 copy-done.1
  4.0 26.0 %shard_map.94 = (f32[8,64,128]{2,1,0:T(8,128)S(1)}, f32[8,64,128]{2,1,0:T(8,128)S(1)}, f32[6,64,128]{2,1,0:T(8,128)S(1)}) custom-call(f32[8,64,128]{2,1,0:T(8,128)S(1)} %copy-done, f32[8,64,128]{2,1,0:T(8,128)S(1)} %copy-done.1, bf16[8,32,128]{2,1,0:T(8,128)(2,1)S(1)} %pad_maximum_fusion.payload_ref, f32[102,256]{1,0:T(8,128)S(1)} %reshape.55.taps_ref, ...), custom_call_target="tpu_custom_call" | custom-call | tf_op jit(solution)/shard_map/pallas_call | solution.py:275
  30.1 0.7 %copy.17 = f32[8,64,128]{2,1,0:T(8,128)} copy(f32[8,64,128]{2,1,0:T(8,128)S(1)} %get-tuple-element.6) | data formatting | bytes 524288
  30.8 0.7 %copy.18 = f32[8,64,128]{2,1,0:T(8,128)} copy(f32[8,64,128]{2,1,0:T(8,128)S(1)} %get-tuple-element.7) | data formatting | bytes 524288
  31.5 0.7 %copy.19 = f32[6,64,128]{2,1,0:T(8,128)} copy(f32[6,64,128]{2,1,0:T(8,128)S(1)} %get-tuple-element.8) | data formatting | bytes 393216
  (4 shorter events, 0.1 us)
Async XLA Ops:
  0.6 0.9 %copy-start.3 = (bf16[1,8,2,8,128]{4,3,2,1,0:T(8,128)(2,1)S(1)}, bf16[1,8,2,8,128]{4,3,2,1,0:T(8,128)(2,1)}, u32[]{:S(2)}) copy-start(bf16[1,8,2,8,128]{4,3,2,1,0:T(8,128)(2,1)} %param.9) | copy-start | bytes 98308
  2.9 0.9 %copy-start.2 = (f32[6,64,128]{2,1,0:T(8,128)S(1)}, f32[6,64,128]{2,1,0:T(8,128)}, u32[]{:S(2)}) copy-start(f32[6,64,128]{2,1,0:T(8,128)} %observed_ref.1) | copy-start | bytes 589828
  2.9 1.0 %copy-start = (f32[8,64,128]{2,1,0:T(8,128)S(1)}, f32[8,64,128]{2,1,0:T(8,128)}, u32[]{:S(2)}) copy-start(f32[8,64,128]{2,1,0:T(8,128)} %density_ref.1) | copy-start | bytes 786436
  2.9 1.1 %copy-start.1 = (f32[8,64,128]{2,1,0:T(8,128)S(1)}, f32[8,64,128]{2,1,0:T(8,128)}, u32[]{:S(2)}) copy-start(f32[8,64,128]{2,1,0:T(8,128)} %sigma_ref.1) | copy-start | bytes 786436

commit v2 on v1

--- a/solution.py
+++ b/solution.py
@@ -31,16 +31,16 @@
 
 
 def body(
-    sizes, density_ref, sigma_ref, payload_ref, taps_ref, observed_ref,
+    sizes, density_ref, sigma_ref, values_in, rows_in, counts_in, taps_in, observed_ref,
     sigma_out, density_out, residual_out,
-    arrived, wide_d, wide_s, pack, sides, flux_z, lateral, rounded, toeplitz, blocks, part, other,
-    all_send, all_recv, z_send, z_recv, near_send, near_recv, sum_send, sum_recv,
+    sigma_in, observed_in, values_ref, rows_ref, counts_ref, taps_ref, payload, arrived, wide_d, wide_s, pack, sides, flux_z, lateral, rounded, toeplitz, blocks, part, other,
+    load_sem, all_send, all_recv, z_send, z_recv, near_send, near_recv, sum_send, sum_recv,
 ):
     n_gx, n_gy, n_gz = sizes
     tiles = n_gx * n_gy
     nz, rows, cols = density_ref.shape
     comps = observed_ref.shape[0]
-    span = taps_ref.shape[0] // comps
+    span = taps_ref.shape[1]
     ext = rows + 2 * EDGE
     ix, iy, iz = lax.axis_index("gx"), lax.axis_index("gy"), lax.axis_index("gz")
     me = ix * n_gy + iy
@@ -54,10 +54,25 @@
         else:
             lax.fori_loop(1, tiles, lambda off, _: (step(off), 0)[1], 0)
 
+    loads = [
+        pltpu.make_async_copy(density_ref, wide_d.at[pl.ds(2, nz), inner, own], load_sem.at[0]),
+        pltpu.make_async_copy(sigma_ref, sigma_in, load_sem.at[1]),
+        pltpu.make_async_copy(observed_ref, observed_in, load_sem.at[2]),
+        pltpu.make_async_copy(values_in, values_ref, load_sem.at[3]),
+        pltpu.make_async_copy(rows_in, rows_ref, load_sem.at[4]),
+        pltpu.make_async_copy(counts_in, counts_ref, load_sem.at[5]),
+        pltpu.make_async_copy(taps_in, taps_ref, load_sem.at[6]),
+    ]
+    for load in loads[3:] + loads[:3]:
+        load.start()
+    for wide in (wide_d, wide_s, rounded):
+        depth = wide.shape[0]
+        for first in (0, EDGE + rows):
+            wide[:, first : first + EDGE, :cols] = jnp.zeros((depth, EDGE, cols), jnp.float32)
     for wide in (wide_d, wide_s):
-        wide[...] = jnp.zeros_like(wide)
+        for first in (0, nz + 2):
+            wide[first : first + 2, inner, own] = jnp.zeros((2, rows, cols), jnp.float32)
     sides[...] = jnp.zeros_like(sides)
-    rounded[...] = jnp.zeros_like(rounded)
 
     barrier = pltpu.get_barrier_semaphore()
 
@@ -70,17 +85,35 @@
     over_tiles(greet)
     for off in range(1, n_gz):
         pl.semaphore_signal(barrier, inc=1, device_id={"gz": lax.rem(iz + off, n_gz)}, device_id_type=MESH)
+
+    slot_row = lax.rem(lax.broadcasted_iota(jnp.int32, (nz, 128), 1), rows)
+
+    def load_blocks(tile):
+        payload[tile, 0:16, :] = values_ref[tile]
+        picked = []
+        for k in range(16 // nz):
+            target = jnp.where(k < counts_ref[0, tile], rows_ref[k, tile], -1)
+            picked.append(jnp.where(slot_row == target, 1.0, 0.0))
+        payload[tile, 16:32, :] = jnp.concatenate(picked, axis=0).astype(jnp.bfloat16)
+
+    for load in loads[3:6]:
+        load.wait()
+    if tiles <= 16:
+        for tile in range(tiles):
+            load_blocks(tile)
+    else:
+        lax.fori_loop(0, tiles, lambda tile, _: (load_blocks(tile), 0)[1], 0)
     pl.semaphore_wait(barrier, tiles - 1 + n_gz - 1)
 
     def block_copy(tile, source):
         return pltpu.make_async_remote_copy(
-            src_ref=payload_ref.at[tile], dst_ref=arrived.at[source],
+            src_ref=payload.at[tile], dst_ref=arrived.at[source],
             send_sem=all_send.at[tile], recv_sem=all_recv.at[source],
             device_id={"gx": tile // n_gy, "gy": lax.rem(tile, n_gy)}, device_id_type=MESH,
         )
 
     over_tiles(lambda off: block_copy(lax.rem(me + off, tiles), me).start())
-    arrived[me] = payload_ref[me]
+    arrived[me] = payload[me]
 
     def z_copy(wide, field, up):
         src, dst = (pl.ds(nz, 2), pl.ds(0, 2)) if up else (pl.ds(2, 2), pl.ds(nz + 2, 2))
@@ -126,8 +159,11 @@
             device_id={"gx": x, "gy": y}, device_id_type=MESH,
         )
 
-    def near_start(wide, field):
+    def near_start(wide, field, faces):
         for at, (dx, dy) in enumerate(STEPS):
+            if (dy == 0) != faces:
+                continue
+
             @pl.when(inside(ix + dx, iy + dy))
             def _():
                 near_copy(wide, field, at, dx, dy, ix + dx, iy + dy).start()
@@ -146,25 +182,38 @@
         for i in range(nz + 4):
             wide[i, :, pl.ds(cols, cols)] = halo_columns(sides[field, 0], sides[field, 1], i, 4)
 
-    wide_d[pl.ds(2, nz), inner, own] = density_ref[...]
+    loads[0].wait()
     z_start(wide_d, 0)
 
-    depth = taps_ref.shape[1]
-    for row in range(span * comps):
-        for half in range(depth // 128):
-            taps = jnp.broadcast_to(taps_ref[row : row + 1, half * 128 : (half + 1) * 128], (16, 128))
-            band = pltpu.roll(taps, 0, 1, stride=1, stride_axis=0)
-            toeplitz[row * 16 : (row + 1) * 16, half * 128 : (half + 1) * 128] = band.astype(jnp.bfloat16)
+    depth = nz * 32
+    place_row = lax.broadcasted_iota(jnp.int32, (span * nz, depth), 0)
+    place_lane = lax.broadcasted_iota(jnp.int32, (span * nz, depth), 1)
+    place = place_lane == lax.rem(place_row, nz) * 32 + place_row // nz
+    place = jnp.where(place, 1.0, 0.0).astype(jnp.bfloat16)
+    loads[6].wait()
+    for c in range(comps):
+        footprint = taps_ref[c].astype(jnp.float32).reshape(span * nz, span).astype(jnp.bfloat16)
+        lines = lax.dot_general(
+            footprint, place, (((0,), (0,)), ((), ())), preferred_element_type=jnp.float32
+        )
+        for b in range(span):
+            first = (b * comps + c) * 16
+            for half in range(depth // 128):
+                taps = jnp.broadcast_to(lines[b : b + 1, half * 128 : (half + 1) * 128], (16, 128))
+                band = pltpu.roll(taps, 0, 1, stride=1, stride_axis=0)
+                toeplitz[first : first + 16, half * 128 : (half + 1) * 128] = band.astype(jnp.bfloat16)
 
     z_finish(wide_d, 0)
+    near_start(wide_d, 0, True)
     pack[0] = packed_columns([wide_d[i, inner, own] for i in range(nz + 4)], 4)
-    near_start(wide_d, 0)
+    near_start(wide_d, 0, False)
 
     def landed(off):
         tile = lax.rem(me + off, tiles)
         copy = block_copy(tile, tile)
         copy.wait_recv()
 
+    loads[1].wait()
     over_tiles(landed)
     slots = tiles * 16
     values = arrived[:, 0:16, :].reshape(slots, cols)
@@ -175,15 +224,16 @@
         chosen = jnp.where(slot_z == row_z + 2 * g, picks, 0.0).astype(jnp.bfloat16)
         total = jnp.dot(chosen, values, preferred_element_type=jnp.float32)
         for j in range(2):
-            trial = sigma_ref[2 * g + j] - 0.5 * total[j * rows : (j + 1) * rows]
+            trial = sigma_in[2 * g + j] - 0.5 * total[j * rows : (j + 1) * rows]
             wide_s[2 * g + j + 2, inner, own] = trial
             sigma_out[2 * g + j] = trial
     z_start(wide_s, 1)
     near_finish(wide_d, 0)
     unpack(wide_d, 0)
     z_finish(wide_s, 1)
+    near_start(wide_s, 1, True)
     pack[1] = packed_columns([wide_s[i, inner, own] for i in range(nz + 4)], 4)
-    near_start(wide_s, 1)
+    near_start(wide_s, 1, False)
     near_finish(wide_s, 1)
     unpack(wide_s, 1)
 
@@ -214,11 +264,12 @@
 
     lax.fori_loop(1, nz + 3, layer, 0)
     for i in range(nz):
-        trial = density_ref[i] + 0.25 * (lateral[i + 2] + (flux_z[i + 3] - flux_z[i + 1]))
+        trial = wide_d[i + 2, inner, own] + 0.25 * (lateral[i + 2] + (flux_z[i + 3] - flux_z[i + 1]))
         density_out[i] = trial
         rounded[i, inner, own] = trial.astype(jnp.bfloat16).astype(jnp.float32)
+    near_start(rounded, 2, True)
     pack[2] = packed_columns([rounded[i, inner, own] for i in range(nz)], 8)
-    near_start(rounded, 2)
+    near_start(rounded, 2, False)
     near_finish(rounded, 2)
     for i in range(nz):
         rounded[i, :, pl.ds(cols, cols)] = halo_columns(sides[2, 0], sides[2, 1], i, 8)
@@ -227,7 +278,14 @@
         for i in range(nz):
             blocks[s, i * 32 : (i + 1) * 32, :] = rounded[i, s * 16 : s * 16 + 32, :].astype(jnp.bfloat16)
 
-    def section(s, _):
+    def swap(s):
+        return pltpu.make_async_remote_copy(
+            src_ref=part.at[:, pl.ds(s * 16, 16), :], dst_ref=other.at[:, pl.ds(s * 16, 16), :],
+            send_sem=sum_send.at[s], recv_sem=sum_recv.at[s],
+            device_id={"gz": n_gz - 1 - iz}, device_id_type=MESH,
+        )
+
+    for s in range(rows // 16):
         block = blocks[s]
         total = jnp.zeros((comps * 16, cols), jnp.float32)
         for b in range(span):
@@ -236,23 +294,19 @@
             )
             total = total + pltpu.roll(one, (8 - b) % (2 * cols), 1)[:, :cols]
         for c in range(comps):
-            part[c, pl.ds(pl.multiple_of(s * 16, 16), 16), :] = total[c * 16 : (c + 1) * 16]
-        return 0
-
-    lax.fori_loop(0, rows // 16, section, 0)
-
-    if n_gz > 1:
-        swap = pltpu.make_async_remote_copy(
-            src_ref=part, dst_ref=other, send_sem=sum_send, recv_sem=sum_recv,
-            device_id={"gz": n_gz - 1 - iz}, device_id_type=MESH,
-        )
-        swap.start()
-        over_tiles(lambda off: block_copy(lax.rem(me + off, tiles), me).wait_send())
-        swap.wait()
-        residual_out[...] = part[...] + other[...] - observed_ref[...]
-    else:
-        over_tiles(lambda off: block_copy(lax.rem(me + off, tiles), me).wait_send())
-        residual_out[...] = part[...] - observed_ref[...]
+            part[c, s * 16 : (s + 1) * 16, :] = total[c * 16 : (c + 1) * 16]
+        if n_gz > 1:
+            swap(s).start()
+
+    loads[2].wait()
+    over_tiles(lambda off: block_copy(lax.rem(me + off, tiles), me).wait_send())
+    for s in range(rows // 16):
+        here = pl.ds(s * 16, 16)
+        if n_gz > 1:
+            swap(s).wait()
+            residual_out[:, here, :] = part[:, here, :] + other[:, here, :] - observed_in[:, here, :]
+        else:
+            residual_out[:, here, :] = part[:, here, :] - observed_in[:, here, :]
 
 
 def local(sizes, density, sigma, mt_values, mt_rows, mt_counts, kernel, observed):
@@ -260,29 +314,27 @@
     tiles, capacity = mt_values.shape[1:3]
     comps, span = kernel.shape[0], kernel.shape[2]
     ext = rows + 2 * EDGE
-    live = jnp.arange(capacity, dtype=jnp.int32)[None, :] < mt_counts[0][:, None]
-    target = jnp.where(live, mt_rows[0], -1)
-    picks = target[:, :, None, None] == jnp.arange(128, dtype=jnp.int32) % rows
-    picks = jnp.broadcast_to(picks, (tiles, capacity, nz, 128)).reshape(tiles, capacity * nz, 128)
-    payload = jnp.concatenate(
-        [mt_values[0].reshape(tiles, capacity * nz, cols), picks.astype(jnp.bfloat16)], axis=1
-    )
-    taps = jnp.pad(kernel.transpose(3, 0, 1, 2), ((0, 0), (0, 0), (0, 0), (0, 32 - span)))
-    taps = taps.reshape(span * comps, nz * 32).astype(jnp.float32)
+    blocks = mt_values[0].reshape(tiles, capacity * nz, cols)
+    taps = kernel.transpose(0, 2, 1, 3)
     vmem = pl.BlockSpec(memory_space=pltpu.VMEM)
+    whole = pl.BlockSpec(memory_space=pltpu.HBM)
     f32 = jnp.float32
     dma = pltpu.SemaphoreType.DMA
+    shapes = tuple(jax.ShapeDtypeStruct(like.shape, f32) for like in (sigma, density, observed))
     return pl.pallas_call(
         functools.partial(body, sizes),
-        out_shape=(
-            jax.ShapeDtypeStruct(sigma.shape, f32),
-            jax.ShapeDtypeStruct(density.shape, f32),
-            jax.ShapeDtypeStruct(observed.shape, f32),
-        ),
-        in_specs=[vmem] * 5,
+        out_shape=shapes,
+        in_specs=[whole] * 7,
         out_specs=(vmem,) * 3,
         scratch_shapes=[
-            pltpu.VMEM(payload.shape, jnp.bfloat16),
+            pltpu.VMEM(sigma.shape, f32),
+            pltpu.VMEM(observed.shape, f32),
+            pltpu.VMEM(blocks.shape, jnp.bfloat16),
+            pltpu.SMEM((capacity, tiles), jnp.int32),
+            pltpu.SMEM((1, tiles), jnp.int32),
+            pltpu.VMEM(taps.shape, jnp.bfloat16),
+            pltpu.VMEM((tiles, 32, 128), jnp.bfloat16),
+            pltpu.VMEM((tiles, 32, 128), jnp.bfloat16),
             pltpu.VMEM((nz + 4, ext, 2 * cols), f32),
             pltpu.VMEM((nz + 4, ext, 2 * cols), f32),
             pltpu.VMEM((3, rows, 128), f32),
@@ -294,13 +346,13 @@
             pltpu.VMEM((rows // 16, nz * 32, 2 * cols), jnp.bfloat16),
             pltpu.VMEM(observed.shape, f32),
             pltpu.VMEM(observed.shape, f32),
-            dma((tiles,)), dma((tiles,)), dma((2, 2)), dma((2, 2)),
-            dma((3, 8)), dma((3, 8)), dma, dma,
+            dma((7,)), dma((tiles,)), dma((tiles,)), dma((2, 2)), dma((2, 2)),
+            dma((3, 8)), dma((3, 8)), dma((rows // 16,)), dma((rows // 16,)),
         ],
         compiler_params=pltpu.CompilerParams(
-            collective_id=0, has_side_effects=True, vmem_limit_bytes=40 * 1024 * 1024
+            collective_id=0, has_side_effects=True, vmem_limit_bytes=57 * 1024 * 1024
         ),
-    )(density, sigma, payload, taps, observed)
+    )(density, sigma, blocks, mt_rows[0].T, mt_counts, taps, observed)
 
 
 def solution(mesh):

time: 32.4 us -> 30.5 us (0.941)
  local copies, waits for them, and re-layouts: 4.61 us -> 3.41 us
  other arithmetic: 0.81 us -> 0 us
    unnamed x12 -> x7, local copies, waits for them, and re-layouts: 4.36 us -> 3.41 us
    select_n x2 -> x0, other arithmetic: 0.69 us -> none  [the longest x1 0.69 us: local(): target = jnp.where(live, mt_rows[0], -1)]
where the time goes in v2:
time: 30.5 us; the launch traced here: 30.3 us
  Pallas kernels  26.3 us (86%)
  local copies, waits for them, and re-layouts  3.41 us (11%)
  between operations  0.65 us (2%)
    pallas_call x1, Pallas kernels, local(): pl.pallas_call(functools.partial(body, sizes), out_shape=shapes, in_specs...  26.3 us
    unnamed x7, local copies, waits for them, and re-layouts  3.41 us

profile of v2, /device:TPU:0, one launch (start us, length us, event | category | flops | bytes accessed | tf_op | source)
XLA Modules:
  0.0 30.3 jit_solution(4578527117455371986)
XLA Ops:
  0.6 26.3 %shard_map.94 = (f32[8,64,128]{2,1,0:T(8,128)}, f32[8,64,128]{2,1,0:T(8,128)}, f32[6,64,128]{2,1,0:T(8,128)}) custom-call(f32[8,64,128]{2,1,0:T(8,128)} %density_ref.1, f32[8,64,128]{2,1,0:T(8,128)} %sigma_ref.1, bf16[8,16,128]{2,1,0:T(8,128)(2,1)} %bitcast.6, s32[2,8]{1,0:T(2,128)} %bitcast.7, s32[1,8]{1,0:T(1,128)} %counts_in.1, ...), custom_call_target="tpu_custom_call" | custom-call | tf_op jit(solution)/shard_map/pallas_call | solution.py:324
  26.9 0.0 copy-start
  26.9 1.7 %copy.13 = f32[8,64,128]{2,1,0:T(8,128)} copy(f32[8,64,128]{2,1,0:T(8,128)} %get-tuple-element.6) | data formatting | bytes 524288
  28.6 0.0 copy-done
  28.6 0.0 copy-start.1
  28.6 0.7 %copy.14 = f32[8,64,128]{2,1,0:T(8,128)} copy(f32[8,64,128]{2,1,0:T(8,128)S(1)} %copy-done) | data formatting | bytes 524288
  29.3 0.3 %copy-done.1 = f32[6,64,128]{2,1,0:T(8,128)S(1)} copy-done((f32[6,64,128]{2,1,0:T(8,128)S(1)}, f32[6,64,128]{2,1,0:T(8,128)}, u32[]{:S(2)}) %copy-start.1) | copy-done | bytes 196632
  29.6 0.7 %copy.15 = f32[6,64,128]{2,1,0:T(8,128)} copy(f32[6,64,128]{2,1,0:T(8,128)S(1)} %copy-done.1) | data formatting | bytes 393216
Async XLA Ops:
  26.9 1.7 %copy-start = (f32[8,64,128]{2,1,0:T(8,128)S(1)}, f32[8,64,128]{2,1,0:T(8,128)}, u32[]{:S(2)}) copy-start(f32[8,64,128]{2,1,0:T(8,128)} %get-tuple-element.7) | copy-start | bytes 786436
  28.6 1.0 %copy-start.1 = (f32[6,64,128]{2,1,0:T(8,128)S(1)}, f32[6,64,128]{2,1,0:T(8,128)}, u32[]{:S(2)}) copy-start(f32[6,64,128]{2,1,0:T(8,128)} %get-tuple-element.8) | copy-start | bytes 589828

commit v3 on v2

--- a/solution.py
+++ b/solution.py
@@ -246,7 +246,7 @@
         size = value.shape[axis]
         return pltpu.roll(value, size - 1, axis) - pltpu.roll(value, 1, axis)
 
-    def layer(i, _):
+    for i in range(1, nz + 3):
         def gradient(wide):
             here = wide[i]
             return shifted(here, 0) * 0.5, shifted(here, 1) * 0.5, (wide[i + 1] - wide[i - 1]) * 0.5
@@ -254,15 +254,18 @@
         dx, dy, dz = gradient(wide_d)
         sx, sy, sz = gradient(wide_s)
         cx, cy, cz = dy * sz - dz * sy, dz * sx - dx * sz, dx * sy - dy * sx
-        fx = jnp.where(row_in, sy * cz - sz * cy, 0.0)
-        fy = jnp.where(lane_in, sz * cx - sx * cz, 0.0)
         fz = sx * cy - sy * cx
-        z_in = ((i >= 2) | has_down) & ((i < nz + 2) | has_up)
-        flux_z[i] = jnp.where(z_in, fz[EDGE : EDGE + rows, :cols], 0.0)
-        lateral[i] = (shifted(fx, 0) + shifted(fy, 1))[EDGE : EDGE + rows, :cols]
-        return 0
-
-    lax.fori_loop(1, nz + 3, layer, 0)
+        fz = fz[EDGE : EDGE + rows, :cols]
+        if i == 1:
+            fz = jnp.where(has_down, fz, 0.0)
+        if i == nz + 2:
+            fz = jnp.where(has_up, fz, 0.0)
+        flux_z[i] = fz
+        if 2 <= i < nz + 2:
+            fx = jnp.where(row_in, sy * cz - sz * cy, 0.0)
+            fy = jnp.where(lane_in, sz * cx - sx * cz, 0.0)
+            lateral[i] = (shifted(fx, 0) + shifted(fy, 1))[EDGE : EDGE + rows, :cols]
+
     for i in range(nz):
         trial = wide_d[i + 2, inner, own] + 0.25 * (lateral[i + 2] + (flux_z[i + 3] - flux_z[i + 1]))
         density_out[i] = trial

time: 30.5 us -> 29.5 us (0.967)
  Pallas kernels: 26.3 us -> 25.3 us
    pallas_call x1, Pallas kernels: 26.3 us -> 25.3 us  [local(): pl.pallas_call(functools.partial(body, sizes), out_shape=shapes, in_specs...]
where the time goes in v3:
time: 29.5 us; the launch traced here: 29.4 us
  Pallas kernels  25.3 us (86%)
  local copies, waits for them, and re-layouts  3.41 us (12%)
  between operations  0.65 us (2%)
    pallas_call x1, Pallas kernels, local(): pl.pallas_call(functools.partial(body, sizes), out_shape=shapes, in_specs...  25.3 us
    unnamed x7, local copies, waits for them, and re-layouts  3.41 us

profile of v3, /device:TPU:0, one launch (start us, length us, event | category | flops | bytes accessed | tf_op | source)
XLA Modules:
  0.0 29.4 jit_solution(9902354999496266273)
XLA Ops:
  0.6 25.3 %shard_map.94 = (f32[8,64,128]{2,1,0:T(8,128)}, f32[8,64,128]{2,1,0:T(8,128)}, f32[6,64,128]{2,1,0:T(8,128)}) custom-call(f32[8,64,128]{2,1,0:T(8,128)} %density_ref.1, f32[8,64,128]{2,1,0:T(8,128)} %sigma_ref.1, bf16[8,16,128]{2,1,0:T(8,128)(2,1)} %bitcast.6, s32[2,8]{1,0:T(2,128)} %bitcast.7, s32[1,8]{1,0:T(1,128)} %counts_in.1, ...), custom_call_target="tpu_custom_call" | custom-call | tf_op jit(solution)/shard_map/pallas_call | solution.py:327
  25.9 0.0 copy-start
  25.9 1.7 %copy.13 = f32[8,64,128]{2,1,0:T(8,128)} copy(f32[8,64,128]{2,1,0:T(8,128)} %get-tuple-element.6) | data formatting | bytes 524288
  27.7 0.0 copy-done
  27.7 0.0 copy-start.1
  27.7 0.7 %copy.14 = f32[8,64,128]{2,1,0:T(8,128)} copy(f32[8,64,128]{2,1,0:T(8,128)S(1)} %copy-done) | data formatting | bytes 524288
  28.4 0.3 %copy-done.1 = f32[6,64,128]{2,1,0:T(8,128)S(1)} copy-done((f32[6,64,128]{2,1,0:T(8,128)S(1)}, f32[6,64,128]{2,1,0:T(8,128)}, u32[]{:S(2)}) %copy-start.1) | copy-done | bytes 196632
  28.7 0.7 %copy.15 = f32[6,64,128]{2,1,0:T(8,128)} copy(f32[6,64,128]{2,1,0:T(8,128)S(1)} %copy-done.1) | data formatting | bytes 393216
Async XLA Ops:
  25.9 1.7 %copy-start = (f32[8,64,128]{2,1,0:T(8,128)S(1)}, f32[8,64,128]{2,1,0:T(8,128)}, u32[]{:S(2)}) copy-start(f32[8,64,128]{2,1,0:T(8,128)} %get-tuple-element.7) | copy-start | bytes 786436
  27.7 1.0 %copy-start.1 = (f32[6,64,128]{2,1,0:T(8,128)S(1)}, f32[6,64,128]{2,1,0:T(8,128)}, u32[]{:S(2)}) copy-start(f32[6,64,128]{2,1,0:T(8,128)} %get-tuple-element.8) | copy-start | bytes 589828

commit v4 on v3

--- a/solution.py
+++ b/solution.py
@@ -32,8 +32,8 @@
 
 def body(
     sizes, density_ref, sigma_ref, values_in, rows_in, counts_in, taps_in, observed_ref,
-    sigma_out, density_out, residual_out,
-    sigma_in, observed_in, values_ref, rows_ref, counts_ref, taps_ref, payload, arrived, wide_d, wide_s, pack, sides, flux_z, lateral, rounded, toeplitz, blocks, part, other,
+    sigma_hbm, density_hbm, residual_out,
+    sigma_out, density_out, sigma_in, observed_in, values_ref, rows_ref, counts_ref, taps_ref, payload, arrived, wide_d, wide_s, pack, sides, flux_z, lateral, rounded, toeplitz, blocks, part, other,
     load_sem, all_send, all_recv, z_send, z_recv, near_send, near_recv, sum_send, sum_recv,
 ):
     n_gx, n_gy, n_gz = sizes
@@ -228,6 +228,11 @@
             wide_s[2 * g + j + 2, inner, own] = trial
             sigma_out[2 * g + j] = trial
     z_start(wide_s, 1)
+    saves = [
+        pltpu.make_async_copy(sigma_out, sigma_hbm, load_sem.at[7]),
+        pltpu.make_async_copy(density_out, density_hbm, load_sem.at[8]),
+    ]
+    saves[0].start()
     near_finish(wide_d, 0)
     unpack(wide_d, 0)
     z_finish(wide_s, 1)
@@ -271,6 +276,7 @@
         density_out[i] = trial
         rounded[i, inner, own] = trial.astype(jnp.bfloat16).astype(jnp.float32)
     near_start(rounded, 2, True)
+    saves[1].start()
     pack[2] = packed_columns([rounded[i, inner, own] for i in range(nz)], 8)
     near_start(rounded, 2, False)
     near_finish(rounded, 2)
@@ -302,6 +308,8 @@
             swap(s).start()
 
     loads[2].wait()
+    for save in saves:
+        save.wait()
     over_tiles(lambda off: block_copy(lax.rem(me + off, tiles), me).wait_send())
     for s in range(rows // 16):
         here = pl.ds(s * 16, 16)
@@ -328,8 +336,10 @@
         functools.partial(body, sizes),
         out_shape=shapes,
         in_specs=[whole] * 7,
-        out_specs=(vmem,) * 3,
+        out_specs=(whole, whole, vmem),
         scratch_shapes=[
+            pltpu.VMEM(sigma.shape, f32),
+            pltpu.VMEM(density.shape, f32),
             pltpu.VMEM(sigma.shape, f32),
             pltpu.VMEM(observed.shape, f32),
             pltpu.VMEM(blocks.shape, jnp.bfloat16),
@@ -349,7 +359,7 @@
             pltpu.VMEM((rows // 16, nz * 32, 2 * cols), jnp.bfloat16),
             pltpu.VMEM(observed.shape, f32),
             pltpu.VMEM(observed.shape, f32),
-            dma((7,)), dma((tiles,)), dma((tiles,)), dma((2, 2)), dma((2, 2)),
+            dma((9,)), dma((tiles,)), dma((tiles,)), dma((2, 2)), dma((2, 2)),
             dma((3, 8)), dma((3, 8)), dma((rows // 16,)), dma((rows // 16,)),
         ],
         compiler_params=pltpu.CompilerParams(

time: 29.5 us -> 29.4 us (level)
  no operation moved by 1% of the time
where the time goes in v4:
time: 29.4 us; the launch traced here: 29.2 us
  Pallas kernels  25.1 us (85%)
  local copies, waits for them, and re-layouts  3.41 us (12%)
  between operations  0.65 us (2%)
    pallas_call x1, Pallas kernels, local(): pl.pallas_call(functools.partial(body, sizes), out_shape=shapes, in_specs...  25.1 us
    unnamed x7, local copies, waits for them, and re-layouts  3.41 us

profile of v4, /device:TPU:0, one launch (start us, length us, event | category | flops | bytes accessed | tf_op | source)
XLA Modules:
  0.0 29.2 jit_solution(4195927305886050069)
XLA Ops:
  0.6 25.1 %shard_map.94 = (f32[8,64,128]{2,1,0:T(8,128)}, f32[8,64,128]{2,1,0:T(8,128)}, f32[6,64,128]{2,1,0:T(8,128)}) custom-call(f32[8,64,128]{2,1,0:T(8,128)} %density_ref.1, f32[8,64,128]{2,1,0:T(8,128)} %sigma_ref.1, bf16[8,16,128]{2,1,0:T(8,128)(2,1)} %bitcast.6, s32[2,8]{1,0:T(2,128)} %bitcast.7, s32[1,8]{1,0:T(1,128)} %counts_in.1, ...), custom_call_target="tpu_custom_call" | custom-call | tf_op jit(solution)/shard_map/pallas_call | solution.py:335
  25.8 0.0 copy-start
  25.8 1.7 %copy.13 = f32[8,64,128]{2,1,0:T(8,128)} copy(f32[8,64,128]{2,1,0:T(8,128)} %get-tuple-element.6) | data formatting | bytes 524288
  27.5 0.0 copy-done
  27.5 0.0 copy-start.1
  27.5 0.7 %copy.14 = f32[8,64,128]{2,1,0:T(8,128)} copy(f32[8,64,128]{2,1,0:T(8,128)S(1)} %copy-done) | data formatting | bytes 524288
  28.2 0.3 %copy-done.1 = f32[6,64,128]{2,1,0:T(8,128)S(1)} copy-done((f32[6,64,128]{2,1,0:T(8,128)S(1)}, f32[6,64,128]{2,1,0:T(8,128)}, u32[]{:S(2)}) %copy-start.1) | copy-done | bytes 196632
  28.5 0.7 %copy.15 = f32[6,64,128]{2,1,0:T(8,128)} copy(f32[6,64,128]{2,1,0:T(8,128)S(1)} %copy-done.1) | data formatting | bytes 393216
Async XLA Ops:
  25.8 1.7 %copy-start = (f32[8,64,128]{2,1,0:T(8,128)S(1)}, f32[8,64,128]{2,1,0:T(8,128)}, u32[]{:S(2)}) copy-start(f32[8,64,128]{2,1,0:T(8,128)} %get-tuple-element.7) | copy-start | bytes 786436
  27.5 1.0 %copy-start.1 = (f32[6,64,128]{2,1,0:T(8,128)S(1)}, f32[6,64,128]{2,1,0:T(8,128)}, u32[]{:S(2)}) copy-start(f32[6,64,128]{2,1,0:T(8,128)} %get-tuple-element.8) | copy-start | bytes 589828
